TPU v7x, 256 devices: a whole 4x4x8 slice. The times are simulated.
256 devices in a mesh: inner: 16 (over x_hi, z), outer: 8 (over x_lo, y), head: 2 (over core).
Axes of the slice: x: 4 (x_hi: 2, x_lo: 2; x = x_hi * 2 + x_lo), y: 4, z: 8, core: 2. Of those that a mesh axis runs over, the one named last changes fastest.
Arguments:
- query_rows: bfloat16 [32768, 2560], P(('inner', 'outer', 'head')), may hold values from -10 to 10
- key_rows: bfloat16 [32768, 2560], P(('inner', 'outer', 'head')), may hold values from -4 to 4
- value_rows: bfloat16 [32768, 2560], P(('inner', 'outer', 'head')), may hold values from -6 to 6
Outputs:
- attended: bfloat16 [32768, 2560], P(('inner', 'outer', 'head'))
All inputs are finite; a program needn't handle non-finite values.
Results may differ from a plain program's by a relative error of at most 0.0054.
Values may be sent and summed in bfloat16 or wider, within the bound.
A program may use at most 64 MiB of HBM per device.

v0:
```python
import math

import jax
import jax.numpy as jnp
from jax import lax
from jax.sharding import PartitionSpec as P

HD = 128
OSTEPS = 2


def shifted(array, axis, by):
    devices = lax.axis_size(axis)
    return lax.ppermute(array, axis, [(i, (i + by) % devices) for i in range(devices)])


def attend_block(carry, block_pair, query_heads):
    running_max, weight_sum, numerator = carry
    row_count, head_count, head_size = query_heads.shape
    key_heads = block_pair[0].reshape(block_pair.shape[1], head_count, head_size)
    value_heads = block_pair[1].reshape(block_pair.shape[1], head_count, head_size)
    scores = jnp.einsum(
        "qhd,khd->qhk", query_heads, key_heads, preferred_element_type=jnp.float32
    ) / math.sqrt(head_size)
    new_max = jnp.maximum(running_max, jnp.max(scores, axis=2))
    rescale = jnp.exp(running_max - new_max)
    exponent = jnp.exp(scores - new_max[:, :, None])
    weight_sum = weight_sum * rescale + jnp.sum(exponent, axis=2)
    product = jnp.einsum(
        "qhk,khd->qhd",
        exponent.astype(jnp.bfloat16),
        value_heads,
        preferred_element_type=jnp.float32,
    )
    numerator = numerator * rescale[:, :, None] + product
    return (new_max, weight_sum, numerator)


def inner_reach(payload):
    reached = [payload]
    current = payload
    current = shifted(current, "inner", 1)
    reached.append(current)
    return reached


def per_device(query_rows, key_rows, value_rows):
    query_block, key_block, value_block = (
        lax.all_to_all(query_rows, "head", split_axis=1, concat_axis=0, tiled=True),
        lax.all_to_all(key_rows, "head", split_axis=1, concat_axis=0, tiled=True),
        lax.all_to_all(value_rows, "head", split_axis=1, concat_axis=0, tiled=True),
    )
    row_count = query_block.shape[0]
    width_dev = query_block.shape[1]
    head_count = width_dev // HD
    query_heads = query_block.reshape(row_count, head_count, HD)
    key_value = jnp.stack([key_block, value_block])
    gathered = []
    outer_list = [key_value]
    outer_step = 1
    outer_list.append(shifted(key_value, "outer", outer_step))
    for inner_group in inner_reach(jnp.stack(outer_list)):
        for outer_step in range(OSTEPS):
            gathered.append(inner_group[outer_step])
    carry = (
        jnp.full((row_count, head_count), -jnp.inf, jnp.float32),
        jnp.zeros((row_count, head_count), jnp.float32),
        jnp.zeros((row_count, head_count, HD), jnp.float32),
    )
    for block_pair in gathered:
        carry = attend_block(carry, block_pair, query_heads)
    result = (carry[2] / carry[1][:, :, None]).reshape(row_count, width_dev).astype(jnp.bfloat16)
    return lax.all_to_all(result, "head", split_axis=0, concat_axis=1, tiled=True)


def solution(mesh):
    return jax.shard_map(
        per_device,
        mesh=mesh,
        in_specs=(
            P(("inner", "outer", "head"), None),
            P(("inner", "outer", "head"), None),
            P(("inner", "outer", "head"), None),
        ),
        out_specs=P(("inner", "outer", "head"), None),
        check_vma=False,
    )
```

profile of v0, /device:TPU:1, one launch (start us, length us, event | category | flops | bytes accessed | tf_op | source)
XLA Modules:
  0.0 143.3 jit_solution(783965357075108272)
XLA Ops:
  0.0 2.2 %copy.55 = bf16[128,2560]{0,1:T(8,128)(2,1)} copy(bf16[128,2560]{1,0:T(8,128)(2,1)} %param.4) | data formatting | bytes 1310720 | tf_op args[1]
  2.2 6.7 %all-to-all-start = ((bf16[128,2,1280]{0,2,1:T(8,128)(2,1)}), bf16[128,2,1280]{0,2,1:T(8,128)(2,1)S(1)}, u32[]{:S(2)}, u32[]{:S(2)}) async-start(bf16[128,2,1280]{0,2,1:T(8,128)(2,1)} %bitcast), calls=%async_computation | async-start | bytes 1310720 | tf_op jit(solution)/shard_map/all_to_all | solution.py:50
  9.0 1.1 copy.61
  10.4 3.9 %all-to-all-start.2 = ((bf16[128,2,1280]{0,2,1:T(8,128)(2,1)}), bf16[128,2,1280]{0,2,1:T(8,128)(2,1)S(1)}, u32[]{:S(2)}, u32[]{:S(2)}) async-start(bf16[128,2,1280]{0,2,1:T(8,128)(2,1)} %bitcast.5), calls=%async_computation.2 | async-start | bytes 1310720 | tf_op jit(solution)/shard_map/all_to_all | solution.py:51
  14.3 5.4 %copy.56 = bf16[2,128,1280]{1,0,2:T(2,128)(2,1)S(1)} copy(bf16[2,128,1280]{1,2,0:T(8,128)(2,1)S(1)} %bitcast.110) | data formatting | bytes 1310720 | tf_op jit(solution)/shard_map/all_to_all | solution.py:50
  20.2 0.9 constant_dynamic-update-slice_fusion.1
  21.1 5.4 %copy.62 = bf16[2,128,1280]{1,0,2:T(2,128)(2,1)S(1)} copy(bf16[2,128,1280]{1,2,0:T(8,128)(2,1)S(1)} %bitcast.111) | data formatting | bytes 1310720 | tf_op jit(solution)/shard_map/all_to_all | solution.py:51
  26.9 0.9 constant_dynamic-update-slice_fusion
  27.8 32.7 %collective-permute-done = bf16[2,256,1280]{1,2,0:T(8,128)(2,1)S(1)} collective-permute-done((bf16[2,256,1280]{1,2,0:T(8,128)(2,1)}, bf16[2,256,1280]{1,2,0:T(8,128)(2,1)S(1)}, u32[]{:S(2)}, u32[]{:S(2)}) %collective-permute-start) | collective-permute-done | bytes 1310752 | tf_op jit(solution)/shard_map/ppermute | solution.py:14
  60.5 3.1 %pad_maximum_fusion = bf16[2,2,256,1280]{2,3,1,0:T(8,128)(2,1)} fusion(bf16[1,2,256,1280]{2,3,1,0:T(8,128)(2,1)S(1)} %bitcast.107, bf16[1,2,256,1280]{2,3,1,0:T(8,128)(2,1)} %bitcast.12), kind=kLoop, calls=%fused_computation | loop fusion | flops 1310720 | bytes 5242880 | tf_op jit(solution)/shard_map/stack | solution.py:62
  63.7 1.1 copy.57
  64.8 5.3 %all-to-all-start.1 = ((bf16[128,2,1280]{0,2,1:T(8,128)(2,1)}), bf16[128,2,1280]{0,2,1:T(8,128)(2,1)}, u32[]{:S(2)}, u32[]{:S(2)}) async-start(bf16[128,2,1280]{0,2,1:T(8,128)(2,1)} %bitcast.2), calls=%async_computation.1 | async-start | bytes 1310720 | tf_op jit(solution)/shard_map/all_to_all | solution.py:49
  70.0 1.3 reshape_squeeze_stack.6
  71.7 5.7 %copy.58 = bf16[2,128,1280]{1,0,2:T(2,128)(2,1)S(1)} copy(bf16[2,128,1280]{1,2,0:T(8,128)(2,1)} %bitcast.3) | data formatting | bytes 1310720 | tf_op jit(solution)/shard_map/all_to_all | solution.py:49
  77.9 1.6 %bitcast_reduce_fusion.3 = (f32[256,10]{0,1:T(8,128)S(1)}, f32[10,256,256]{2,1,0:T(8,128)S(1)}) fusion(bf16[256,10,128]{0,2,1:T(8,128)(2,1)} %reshape_squeeze_stack.6, bf16[256,10,128]{0,2,1:T(8,128)(2,1)S(1)} %reshape.105), kind=kOutput, calls=%fused_computation.11 | convolution fusion | flops 169080320 | bytes 3942400 | tf_op jit(solution)/shard_map/qhd,khd->qhk/dot_general | solution.py:22
  80.2 46.4 %collective-permute-done.1 = bf16[2,2,256,1280]{2,3,1,0:T(8,128)(2,1)} collective-permute-done((bf16[2,2,256,1280]{2,3,1,0:T(8,128)(2,1)}, bf16[2,2,256,1280]{2,3,1,0:T(8,128)(2,1)}, u32[]{:S(2)}, u32[]{:S(2)}) %collective-permute-start.1) | collective-permute-done | bytes 2621472 | tf_op jit(solution)/shard_map/ppermute | solution.py:14
  126.6 1.8 %fusion.38 = (bf16[1,1,256,1280]{2,3,1,0:T(8,128)(2,1)S(1)}, bf16[1,1,256,1280]{2,3,1,0:T(8,128)(2,1)S(1)}, bf16[1,1,256,1280]{2,3,1,0:T(8,128)(2,1)S(1)}, bf16[1,1,256,1280]{2,3,1,0:T(8,128)(2,1)S(1)}) fusion(bf16[2,2,256,1280]{2,3,1,0:T(8,128)(2,1)} %collective-permute-done.1), kind=kLoop, calls=%fused_computation.54 | loop fusion | bytes 5242880 | tf_op jit(solution)/shard_map/slice | solution.py:21
  129.6 0.9 fusion.4
  131.2 0.7 convolution_bitcast_fusion.1
  131.9 0.9 fusion.6
  132.9 1.6 %fusion.18 = f32[256,10,128]{2,0,1:T(8,128)S(1)} fusion(bf16[256,10,128]{0,2,1:T(8,128)(2,1)S(1)} %reshape_squeeze_stack.7, f32[10,256,256]{2,1,0:T(8,128)S(1)} %get-tuple-element.24, f32[256,10]{0,1:T(8,128)S(1)} %get-tuple-element.23, f32[256,10]{0,1:T(8,128)S(1)} %get-tuple-element.8, f32[256,10]{0,1:T(8,128)S(1)} %get-tuple-element.18), kind=kOutput, calls=%fused_computation.31 | convolution fusion | flops 170393600 | bytes 4618240 | tf_op jit(solution)/shard_map/qhk,khd->qhd/dot_general | solution.py:29
  134.5 1.9 %fusion.20 = bf16[256,10,128]{2,0,1:T(8,128)(2,1)S(1)} fusion(f32[256,10,128]{2,0,1:T(8,128)S(1)} %convolution_bitcast_fusion, f32[256,10,128]{2,0,1:T(8,128)S(1)} %convolution_bitcast_fusion.1, f32[256,10,128]{2,0,1:T(8,128)S(1)} %fusion.18, bf16[256,10,128]{0,2,1:T(8,128)(2,1)S(1)} %bitcast.116, f32[10,256,256]{2,1,0:T(8,128)S(1)} %get-tuple-element.26, ...), kind=kOutput, calls=%fused_computation.33 | convolution fusion | flops 172032000 | bytes 7905280 | tf_op jit(solution)/shard_map/qhk,khd->qhd/dot_general | solution.py:29
  137.0 5.3 %all_to_all.64 = bf16[2,128,1280]{1,2,0:T(8,128)(2,1)S(1)} all-to-all(bf16[2,128,1280]{1,2,0:T(8,128)(2,1)S(1)} %copy.80), channel_id=1, replica_groups=mesh['inner'=16,'outer'=8,'head'=2] {'head'}, dimensions={0} | all-to-all | bytes 1310720 | tf_op jit(solution)/shard_map/all_to_all | solution.py:73
  142.3 1.1 copy.81
  (23 shorter events, 5.2 us)
Async XLA Ops:
  0.0 9.0 %copy-start = (bf16[128,2560]{1,0:T(8,128)(2,1)S(1)}, bf16[128,2560]{1,0:T(8,128)(2,1)}, u32[]{:S(2)}) copy-start(bf16[128,2560]{1,0:T(8,128)(2,1)} %param.5) | copy-start | bytes 1966084
  2.2 8.2 %all-to-all-start = ((bf16[128,2,1280]{0,2,1:T(8,128)(2,1)}), bf16[128,2,1280]{0,2,1:T(8,128)(2,1)S(1)}, u32[]{:S(2)}, u32[]{:S(2)}) async-start(bf16[128,2,1280]{0,2,1:T(8,128)(2,1)} %bitcast), calls=%async_computation | async-start | bytes 1310720 | tf_op jit(solution)/shard_map/all_to_all | solution.py:50
  10.4 10.6 %all-to-all-start.2 = ((bf16[128,2,1280]{0,2,1:T(8,128)(2,1)}), bf16[128,2,1280]{0,2,1:T(8,128)(2,1)S(1)}, u32[]{:S(2)}, u32[]{:S(2)}) async-start(bf16[128,2,1280]{0,2,1:T(8,128)(2,1)} %bitcast.5), calls=%async_computation.2 | async-start | bytes 1310720 | tf_op jit(solution)/shard_map/all_to_all | solution.py:51
  27.8 32.7 %collective-permute-start = (bf16[2,256,1280]{1,2,0:T(8,128)(2,1)}, bf16[2,256,1280]{1,2,0:T(8,128)(2,1)S(1)}, u32[]{:S(2)}, u32[]{:S(2)}) collective-permute-start(bf16[2,256,1280]{1,2,0:T(8,128)(2,1)} %constant_dynamic-update-slice_fusion), channel_id=1, source_target_pairs={{0,2},{2,4},{4,6},{6,8},{8,10},{10,12},{12,14},{14,0},{1,3},{3,5},... | collective-permute-start | bytes 3932168 | tf_op jit(solution)/shard_map/ppermute | solution.py:14
  60.5 3.2 %copy-start.1 = (bf16[128,2560]{1,0:T(8,128)(2,1)S(1)}, bf16[128,2560]{1,0:T(8,128)(2,1)}, u32[]{:S(2)}) copy-start(bf16[128,2560]{1,0:T(8,128)(2,1)} %param.3) | copy-start | bytes 1966084
  63.6 63.0 %collective-permute-start.1 = (bf16[2,2,256,1280]{2,3,1,0:T(8,128)(2,1)}, bf16[2,2,256,1280]{2,3,1,0:T(8,128)(2,1)}, u32[]{:S(2)}, u32[]{:S(2)}) collective-permute-start(bf16[2,2,256,1280]{2,3,1,0:T(8,128)(2,1)} %pad_maximum_fusion), channel_id=1, source_target_pairs={{0,16},{16,32},{32,48},{48,64},{64,80},{80,96},{96,112},{112,128},... | collective-permute-start | bytes 7864328 | tf_op jit(solution)/shard_map/ppermute | solution.py:14
  64.8 6.9 %all-to-all-start.1 = ((bf16[128,2,1280]{0,2,1:T(8,128)(2,1)}), bf16[128,2,1280]{0,2,1:T(8,128)(2,1)}, u32[]{:S(2)}, u32[]{:S(2)}) async-start(bf16[128,2,1280]{0,2,1:T(8,128)(2,1)} %bitcast.2), calls=%async_computation.1 | async-start | bytes 1310720 | tf_op jit(solution)/shard_map/all_to_all | solution.py:49
where the time goes:
time: 144 us; the launch traced here: 143 us
  waiting for transfers between devices  79.5 us (55%)
  local copies, waits for them, and re-layouts  29.2 us (20%)
  starting transfers between devices  16 us (11%)
  matrix products  8.26 us (6%)
  blocking collectives  5.3 us (4%)
  other arithmetic  5.01 us (3%)
    ppermute x2, waiting for transfers between devices, shifted(): lax.ppermute(array, axis, [(i, (i + by) % devices) for i in range(devices)])  79.1 us
    all_to_all x1, starting transfers between devices, per_device(): lax.all_to_all(key_rows, 'head', split_axis=1, concat_axis=0, tiled=True)  6.74 us
    all_to_all x1, local copies, waits for them, and re-layouts, per_device(): lax.all_to_all(query_rows, 'head', split_axis=1, concat_axis=0, tiled=True)  5.74 us
    all_to_all x1, local copies, waits for them, and re-layouts, per_device(): lax.all_to_all(value_rows, 'head', split_axis=1, concat_axis=0, tiled=True)  5.41 us
    all_to_all x1, local copies, waits for them, and re-layouts, per_device(): lax.all_to_all(key_rows, 'head', split_axis=1, concat_axis=0, tiled=True)  5.41 us
    all_to_all x1, blocking collectives, per_device(): lax.all_to_all(result, 'head', split_axis=0, concat_axis=1, tiled=True)  5.3 us
    unnamed x8, local copies, waits for them, and re-layouts  5.27 us
    all_to_all x1, starting transfers between devices, per_device(): lax.all_to_all(query_rows, 'head', split_axis=1, concat_axis=0, tiled=True)  5.26 us
  transfers between devices with their start and end apart: 5, of which 3 were waited for; matrix products, arithmetic and copies ran while one was open for 13% of the time, Pallas kernels for 0%

commit v1 on v0

v1 whole, which is shorter than its diff:
```python
import functools
import math

import jax
import jax.numpy as jnp
from jax import lax
from jax.experimental import pallas as pl
from jax.experimental.pallas import tpu as pltpu
from jax.sharding import PartitionSpec as P

HD = 128
MESH = pl.DeviceIdType.MESH
LANE = 128
TAIL = 16
LAG = 2


def cols(at, count=1):
    return pl.ds(pl.multiple_of(at * HD, HD), count * HD)


def halves(at):
    return pl.ds(pl.multiple_of(at * LANE, LANE), LANE)


def split_sum(x):
    high = x.astype(jnp.bfloat16)
    rest = x - high.astype(jnp.float32)
    mid = rest.astype(jnp.bfloat16)
    low = (rest - mid.astype(jnp.float32)).astype(jnp.bfloat16)
    row = lax.broadcasted_iota(jnp.int32, (TAIL, x.shape[1]), 0)
    wide = [jnp.broadcast_to(part.astype(jnp.float32), (TAIL, x.shape[1])) for part in (high, mid, low)]
    tile = jnp.where(row == 0, wide[0], jnp.where(row == 1, wide[1], jnp.where(row == 2, wide[2], 0.0)))
    return tile.astype(jnp.bfloat16)


def kernel(
    n_inner, n_outer, heads,
    q_hbm, k_hbm, v_hbm, o_hbm,
    q_all, kv_own, kv_far, o_out, o_mine, part_own, part_far, result,
    own_sem, swap_send, swap_recv, q_send, q_recv, kv_send, kv_recv,
    far_send, far_recv, mine_send, mine_recv, out_sem,
):
    inner, outer, core = lax.axis_index("inner"), lax.axis_index("outer"), lax.axis_index("head")
    rows = q_hbm.shape[0]
    other = 1 - core
    inner_up, inner_down = lax.rem(inner + 1, n_inner), lax.rem(inner + n_inner - 1, n_inner)
    outer_up, outer_down = lax.rem(outer + 1, n_outer), lax.rem(outer + n_outer - 1, n_outer)
    my_rows = pl.ds(pl.multiple_of(core * rows, rows), rows)

    own = []
    for at, (src, dst) in enumerate(((q_hbm, q_all.at[0]), (k_hbm, kv_own.at[0]), (v_hbm, kv_own.at[1]))):
        copy = pltpu.make_async_copy(src.at[:, cols(core * heads, heads)], dst.at[my_rows, :], own_sem.at[at])
        copy.start()
        own.append(copy)

    barrier = pltpu.get_barrier_semaphore()
    greeted = [(inner, outer, other)]
    for c in range(2):
        greeted += [(inner_up, outer, c), (inner_down, outer, c), (inner, outer_up, c), (inner, outer_down, c)]
    for device in greeted:
        pl.semaphore_signal(barrier, inc=1, device_id=device, device_id_type=MESH)
    pl.semaphore_wait(barrier, len(greeted))

    swaps = []
    for at, (src, dst) in enumerate(((q_hbm, q_all.at[0]), (k_hbm, kv_own.at[0]), (v_hbm, kv_own.at[1]))):
        copy = pltpu.make_async_remote_copy(
            src_ref=src.at[:, cols(other * heads, heads)], dst_ref=dst.at[my_rows, :],
            send_sem=swap_send.at[at], recv_sem=swap_recv.at[at],
            device_id=(inner, outer, other), device_id_type=MESH,
        )
        copy.start()
        swaps.append(copy)

    def send_head(j, _):
        for c in range(2):
            pltpu.make_async_remote_copy(
                src_ref=q_hbm.at[:, cols(c * heads + j)], dst_ref=q_all.at[1, my_rows, cols(j)],
                send_sem=q_send, recv_sem=q_recv.at[j],
                device_id=(inner_down, outer, c), device_id_type=MESH,
            ).start()
        for at, src in enumerate((k_hbm, v_hbm)):
            for c in range(2):
                pltpu.make_async_remote_copy(
                    src_ref=src.at[:, cols(c * heads + j)], dst_ref=kv_far.at[at, my_rows, cols(j)],
                    send_sem=kv_send.at[at], recv_sem=kv_recv.at[j],
                    device_id=(inner, outer_up, c), device_id_type=MESH,
                ).start()
        return 0

    lax.fori_loop(0, heads, send_head, 0)

    for copy in own:
        copy.wait()
    for copy in swaps:
        copy.wait()

    factor = math.log2(math.e) / math.sqrt(HD)

    def attend(q, j):
        keys = (kv_own[0, :, cols(j)], kv_far[0, :, cols(j)])
        values = (kv_own[1, :, cols(j)], kv_far[1, :, cols(j)])
        scores = [
            lax.dot_general(k, q, (((1,), (1,)), ((), ())), preferred_element_type=jnp.float32) for k in keys
        ]
        top = jnp.max(jnp.maximum(scores[0], scores[1]), axis=0, keepdims=True)
        weights = [jnp.exp2((s - top) * factor) for s in scores]
        total = jnp.sum(weights[0] + weights[1], axis=0, keepdims=True)
        summed = sum(
            lax.dot_general(
                v, w.astype(jnp.bfloat16), (((0,), (0,)), ((), ())), preferred_element_type=jnp.float32
            )
            for v, w in zip(values, weights)
        )
        return (summed * (1.0 / total)).astype(jnp.bfloat16), split_sum(top * factor + jnp.log2(total))

    def merge(j):
        for c in range(2):
            g = c * heads + j
            pltpu.make_async_copy(part_far.at[g], part_far.at[g], far_recv.at[g]).wait()

        pltpu.make_async_copy(
            part_own.at[other * heads + j], part_own.at[other * heads + j], mine_recv.at[j]
        ).wait()
        for c in range(2):
            g = c * heads + j
            logs = []
            for part in (part_own, part_far):
                tile = part[g, HD:, :].astype(jnp.float32)
                logs.append(tile[0:1] + tile[1:2] + tile[2:3])
            share_own = 1.0 / (1.0 + jnp.exp2(logs[1] - logs[0]))
            share_far = 1.0 / (1.0 + jnp.exp2(logs[0] - logs[1]))
            mixed = (
                part_own[g, :HD, :].astype(jnp.float32) * share_own
                + part_far[g, :HD, :].astype(jnp.float32) * share_far
            )
            result[:, cols(g)] = mixed.T.astype(jnp.bfloat16)
            pltpu.make_async_copy(result.at[:, cols(g)], o_hbm.at[:, cols(g)], out_sem).start()

    def head_step(j, _):
        pltpu.make_async_copy(q_all.at[1, :, cols(j)], q_all.at[1, :, cols(j)], q_recv.at[j]).wait()
        pltpu.make_async_copy(kv_far.at[:, :, cols(j)], kv_far.at[:, :, cols(j)], kv_recv.at[j]).wait()
        g = core * heads + j
        block, logs = attend(q_all[1, :, cols(j)], j)
        o_out[j, :HD, :] = block
        o_out[j, HD:, :] = logs
        for c in range(2):
            pltpu.make_async_remote_copy(
                src_ref=o_out.at[j, :, halves(c)], dst_ref=part_far.at[g],
                send_sem=far_send, recv_sem=far_recv.at[g],
                device_id=(inner_up, outer, c), device_id_type=MESH,
            ).start()
        block, logs = attend(q_all[0, :, cols(j)], j)
        o_mine[j, :HD, :] = block
        o_mine[j, HD:, :] = logs
        pltpu.make_async_remote_copy(
            src_ref=o_mine.at[j, :, halves(other)], dst_ref=part_own.at[g],
            send_sem=mine_send, recv_sem=mine_recv.at[j],
            device_id=(inner, outer, other), device_id_type=MESH,
        ).start()
        part_own[g] = o_mine[j, :, halves(core)]

        @pl.when(j >= LAG)
        def _():
            merge(j - LAG)

        return 0

    lax.fori_loop(0, heads, head_step, 0)
    for j in range(heads - LAG, heads):
        merge(j)

    pltpu.make_async_copy(result, o_hbm, out_sem).wait()
    pltpu.make_async_copy(q_hbm, q_hbm, q_send).wait()
    pltpu.make_async_copy(k_hbm, k_hbm, kv_send.at[0]).wait()
    pltpu.make_async_copy(v_hbm, v_hbm, kv_send.at[1]).wait()
    pltpu.make_async_copy(o_out, o_out, far_send).wait()
    pltpu.make_async_copy(o_mine.at[:, :, halves(0)], o_mine.at[:, :, halves(0)], mine_send).wait()


def solution(mesh):
    n_inner, n_outer = mesh.shape["inner"], mesh.shape["outer"]

    def per_device(q, k, v):
        rows, width = q.shape
        heads = width // HD // 2
        both = 2 * rows
        dma = pltpu.SemaphoreType.DMA
        return pl.pallas_call(
            functools.partial(kernel, n_inner, n_outer, heads),
            out_shape=jax.ShapeDtypeStruct((rows, width), jnp.bfloat16),
            in_specs=[pl.BlockSpec(memory_space=pl.ANY)] * 3,
            out_specs=pl.BlockSpec(memory_space=pl.ANY),
            scratch_shapes=[
                pltpu.VMEM((2, both, width // 2), jnp.bfloat16),
                pltpu.VMEM((2, both, width // 2), jnp.bfloat16),
                pltpu.VMEM((2, both, width // 2), jnp.bfloat16),
                pltpu.VMEM((heads, HD + TAIL, both), jnp.bfloat16),
                pltpu.VMEM((heads, HD + TAIL, both), jnp.bfloat16),
                pltpu.VMEM((2 * heads, HD + TAIL, rows), jnp.bfloat16),
                pltpu.VMEM((2 * heads, HD + TAIL, rows), jnp.bfloat16),
                pltpu.VMEM((rows, width), jnp.bfloat16),
                dma((3,)), dma((3,)), dma((3,)),
                dma, dma((heads,)), dma((2,)), dma((heads,)),
                dma, dma((2 * heads,)), dma, dma((heads,)), dma,
            ],
            compiler_params=pltpu.CompilerParams(
                collective_id=0, has_side_effects=True, vmem_limit_bytes=32 << 20
            ),
        )(q, k, v)

    spec = P(("inner", "outer", "head"), None)
    return jax.shard_map(per_device, mesh=mesh, in_specs=(spec,) * 3, out_specs=spec, check_vma=False)
```

time: 144 us -> 65 us (0.45)
  waiting for transfers between devices: 79.5 us -> 0 us
  Pallas kernels: 0 us -> 60.7 us
  local copies, waits for them, and re-layouts: 29.2 us -> 4.1 us
  starting transfers between devices: 16 us -> 0 us
  matrix products: 8.26 us -> 0 us
  blocking collectives: 5.3 us -> 0 us
  other arithmetic: 5.01 us -> 0 us
    ppermute x2 -> x0, waiting for transfers between devices: 79.1 us -> none  [shifted(): lax.ppermute(array, axis, [(i, (i + by) % devices) for i in range(devices)])]
    pallas_call x0 -> x1, Pallas kernels: none -> 60.7 us  [per_device(): pl.pallas_call(functools.partial(kernel, n_inner, n_outer, heads), out_sh...]
    all_to_all x4 -> x0, local copies, waits for them, and re-layouts: 17.7 us -> none  [the longest x1 5.74 us: per_device(): lax.all_to_all(query_rows, 'head', split_axis=1, concat_axis=0, tiled=True)]
    all_to_all x3 -> x0, starting transfers between devices: 15.9 us -> none  [the longest x1 6.74 us: per_device(): lax.all_to_all(key_rows, 'head', split_axis=1, concat_axis=0, tiled=True)]
    dot_general x8 -> x0, matrix products: 8.26 us -> none  [the longest x4 4.92 us: attend_block(): jnp.einsum('qhk,khd->qhd', exponent.astype(jnp.bfloat16), value_heads, pr...]
    all_to_all x1 -> x0, blocking collectives: 5.3 us -> none  [per_device(): lax.all_to_all(result, 'head', split_axis=0, concat_axis=1, tiled=True)]
    another operation x5 -> x0, local copies, waits for them, and re-layouts: 3.39 us -> none  [the longest x3 1.72 us: per_device(): key_value = jnp.stack([key_block, value_block])]
    another operation x1 -> x0, other arithmetic: 3.13 us -> none  [per_device(): jnp.stack(outer_list)]
  transfers between devices with their start and end apart: 5 -> 0, of which waited for: 3 -> 0; matrix products, arithmetic and copies ran while one was open for 13% -> 0% of each run, Pallas kernels for 0% -> 0%
where the time goes in v1:
time: 65 us; the launch traced here: 64.8 us
  Pallas kernels  60.7 us (93%)
  local copies, waits for them, and re-layouts  4.1 us (6%)
    pallas_call x1, Pallas kernels, per_device(): pl.pallas_call(functools.partial(kernel, n_inner, n_outer, heads), out_sh...  60.7 us
    unnamed x7, local copies, waits for them, and re-layouts  4.1 us

profile of v1, /device:TPU:1, one launch (start us, length us, event | category | flops | bytes accessed | tf_op | source)
XLA Modules:
  0.0 64.8 jit_solution(7352527098929534130)
XLA Ops:
  0.0 0.0 copy-start
  0.0 1.1 %copy-done = bf16[128,2560]{1,0:T(8,128)(2,1)S(1)} copy-done((bf16[128,2560]{1,0:T(8,128)(2,1)S(1)}, bf16[128,2560]{1,0:T(8,128)(2,1)}, u32[]{:S(2)}) %copy-start) | copy-done | bytes 655384
  1.1 0.0 copy-start.1
  1.1 1.1 %copy-done.1 = bf16[128,2560]{1,0:T(8,128)(2,1)S(1)} copy-done((bf16[128,2560]{1,0:T(8,128)(2,1)S(1)}, bf16[128,2560]{1,0:T(8,128)(2,1)}, u32[]{:S(2)}) %copy-start.1) | copy-done | bytes 655384
  2.2 0.0 copy-start.2
  2.2 1.1 %copy-done.2 = bf16[128,2560]{1,0:T(8,128)(2,1)S(1)} copy-done((bf16[128,2560]{1,0:T(8,128)(2,1)S(1)}, bf16[128,2560]{1,0:T(8,128)(2,1)}, u32[]{:S(2)}) %copy-start.2) | copy-done | bytes 655384
  3.3 60.7 %shard_map.37 = bf16[128,2560]{1,0:T(8,128)(2,1)S(1)} custom-call(bf16[128,2560]{1,0:T(8,128)(2,1)S(1)} %copy-done, bf16[128,2560]{1,0:T(8,128)(2,1)S(1)} %copy-done.1, bf16[128,2560]{1,0:T(8,128)(2,1)S(1)} %copy-done.2), custom_call_target="tpu_custom_call" | custom-call | tf_op jit(solution)/shard_map/pallas_call | solution.py:189
  63.9 0.8 %copy.5 = bf16[128,2560]{1,0:T(8,128)(2,1)} copy(bf16[128,2560]{1,0:T(8,128)(2,1)S(1)} %shard_map.37) | data formatting | bytes 1310720
Async XLA Ops:
  0.0 1.1 %copy-start = (bf16[128,2560]{1,0:T(8,128)(2,1)S(1)}, bf16[128,2560]{1,0:T(8,128)(2,1)}, u32[]{:S(2)}) copy-start(bf16[128,2560]{1,0:T(8,128)(2,1)} %q_hbm.1) | copy-start | bytes 1966084
  1.1 1.1 %copy-start.1 = (bf16[128,2560]{1,0:T(8,128)(2,1)S(1)}, bf16[128,2560]{1,0:T(8,128)(2,1)}, u32[]{:S(2)}) copy-start(bf16[128,2560]{1,0:T(8,128)(2,1)} %k_hbm.1) | copy-start | bytes 1966084
  2.2 1.1 %copy-start.2 = (bf16[128,2560]{1,0:T(8,128)(2,1)S(1)}, bf16[128,2560]{1,0:T(8,128)(2,1)}, u32[]{:S(2)}) copy-start(bf16[128,2560]{1,0:T(8,128)(2,1)} %v_hbm.1) | copy-start | bytes 1966084

commit v2 on v1

--- a/solution.py
+++ b/solution.py
@@ -37,8 +37,8 @@
 def kernel(
     n_inner, n_outer, heads,
     q_hbm, k_hbm, v_hbm, o_hbm,
-    q_all, kv_own, kv_far, o_out, o_mine, part_own, part_far, result,
-    own_sem, swap_send, swap_recv, q_send, q_recv, kv_send, kv_recv,
+    q_all, kv_own, kv_in, o_out, o_mine, part_own, part_far, result,
+    own_sem, swap_send, swap_recv, q_send, q_recv, kv_send, kv_recv, pass_send,
     far_send, far_recv, mine_send, mine_recv, out_sem,
 ):
     inner, outer, core = lax.axis_index("inner"), lax.axis_index("outer"), lax.axis_index("head")
@@ -46,6 +46,11 @@
     other = 1 - core
     inner_up, inner_down = lax.rem(inner + 1, n_inner), lax.rem(inner + n_inner - 1, n_inner)
     outer_up, outer_down = lax.rem(outer + 1, n_outer), lax.rem(outer + n_outer - 1, n_outer)
+    along = n_outer // 2
+    side, y = outer // along, lax.rem(outer, along)
+    flipped = (1 - side) * along + y
+    ring_up, ring_down = side * along + lax.rem(y + 1, along), side * along + lax.rem(y + along - 1, along)
+    kv_far = kv_in.at[0]
     my_rows = pl.ds(pl.multiple_of(core * rows, rows), rows)
 
     own = []
@@ -58,6 +63,7 @@
     greeted = [(inner, outer, other)]
     for c in range(2):
         greeted += [(inner_up, outer, c), (inner_down, outer, c), (inner, outer_up, c), (inner, outer_down, c)]
+        greeted += [(inner, ring_up, c), (inner, ring_down, c), (inner, flipped, c)]
     for device in greeted:
         pl.semaphore_signal(barrier, inc=1, device_id=device, device_id_type=MESH)
     pl.semaphore_wait(barrier, len(greeted))
@@ -79,12 +85,14 @@
                 send_sem=q_send, recv_sem=q_recv.at[j],
                 device_id=(inner_down, outer, c), device_id_type=MESH,
             ).start()
+        by_ring = jnp.where((y == along - 1) & (lax.rem(j, 2) == 0), 1, 0)
+        target = jnp.where(by_ring == 1, ring_up, outer_up)
         for at, src in enumerate((k_hbm, v_hbm)):
             for c in range(2):
                 pltpu.make_async_remote_copy(
-                    src_ref=src.at[:, cols(c * heads + j)], dst_ref=kv_far.at[at, my_rows, cols(j)],
-                    send_sem=kv_send.at[at], recv_sem=kv_recv.at[j],
-                    device_id=(inner, outer_up, c), device_id_type=MESH,
+                    src_ref=src.at[:, cols(c * heads + j)], dst_ref=kv_in.at[by_ring, at, my_rows, cols(j)],
+                    send_sem=kv_send.at[at], recv_sem=kv_recv.at[by_ring, j],
+                    device_id=(inner, target, c), device_id_type=MESH,
                 ).start()
         return 0
 
@@ -98,8 +106,8 @@
     factor = math.log2(math.e) / math.sqrt(HD)
 
     def attend(q, j):
-        keys = (kv_own[0, :, cols(j)], kv_far[0, :, cols(j)])
-        values = (kv_own[1, :, cols(j)], kv_far[1, :, cols(j)])
+        keys = (kv_own[0, :, cols(j)], kv_in[0, 0, :, cols(j)])
+        values = (kv_own[1, :, cols(j)], kv_in[0, 1, :, cols(j)])
         scores = [
             lax.dot_general(k, q, (((1,), (1,)), ((), ())), preferred_element_type=jnp.float32) for k in keys
         ]
@@ -138,8 +146,17 @@
             pltpu.make_async_copy(result.at[:, cols(g)], o_hbm.at[:, cols(g)], out_sem).start()
 
     def head_step(j, _):
+        @pl.when((y == 0) & (lax.rem(j, 2) == 0))
+        def _():
+            passing = kv_in.at[1, :, :, cols(j)]
+            pltpu.make_async_copy(passing, passing, kv_recv.at[1, j]).wait()
+            pltpu.make_async_remote_copy(
+                src_ref=passing, dst_ref=kv_far.at[:, :, cols(j)], send_sem=pass_send, recv_sem=kv_recv.at[0, j],
+                device_id=(inner, flipped, core), device_id_type=MESH,
+            ).start()
+
         pltpu.make_async_copy(q_all.at[1, :, cols(j)], q_all.at[1, :, cols(j)], q_recv.at[j]).wait()
-        pltpu.make_async_copy(kv_far.at[:, :, cols(j)], kv_far.at[:, :, cols(j)], kv_recv.at[j]).wait()
+        pltpu.make_async_copy(kv_far.at[:, :, cols(j)], kv_far.at[:, :, cols(j)], kv_recv.at[0, j]).wait()
         g = core * heads + j
         block, logs = attend(q_all[1, :, cols(j)], j)
         o_out[j, :HD, :] = block
@@ -175,6 +192,12 @@
     pltpu.make_async_copy(k_hbm, k_hbm, kv_send.at[0]).wait()
     pltpu.make_async_copy(v_hbm, v_hbm, kv_send.at[1]).wait()
     pltpu.make_async_copy(o_out, o_out, far_send).wait()
+
+    @pl.when(y == 0)
+    def _():
+        passed = kv_in.at[1, :, :, cols(0, (heads + 1) // 2)]
+        pltpu.make_async_copy(passed, passed, pass_send).wait()
+
     pltpu.make_async_copy(o_mine.at[:, :, halves(0)], o_mine.at[:, :, halves(0)], mine_send).wait()
 
 
@@ -189,23 +212,23 @@
         return pl.pallas_call(
             functools.partial(kernel, n_inner, n_outer, heads),
             out_shape=jax.ShapeDtypeStruct((rows, width), jnp.bfloat16),
-            in_specs=[pl.BlockSpec(memory_space=pl.ANY)] * 3,
+            in_specs=[pl.BlockSpec(memory_space=pltpu.HBM)] * 3,
             out_specs=pl.BlockSpec(memory_space=pl.ANY),
             scratch_shapes=[
                 pltpu.VMEM((2, both, width // 2), jnp.bfloat16),
                 pltpu.VMEM((2, both, width // 2), jnp.bfloat16),
-                pltpu.VMEM((2, both, width // 2), jnp.bfloat16),
+                pltpu.VMEM((2, 2, both, width // 2), jnp.bfloat16),
                 pltpu.VMEM((heads, HD + TAIL, both), jnp.bfloat16),
                 pltpu.VMEM((heads, HD + TAIL, both), jnp.bfloat16),
                 pltpu.VMEM((2 * heads, HD + TAIL, rows), jnp.bfloat16),
                 pltpu.VMEM((2 * heads, HD + TAIL, rows), jnp.bfloat16),
                 pltpu.VMEM((rows, width), jnp.bfloat16),
                 dma((3,)), dma((3,)), dma((3,)),
-                dma, dma((heads,)), dma((2,)), dma((heads,)),
+                dma, dma((heads,)), dma((2,)), dma((2, heads)), dma,
                 dma, dma((2 * heads,)), dma, dma((heads,)), dma,
             ],
             compiler_params=pltpu.CompilerParams(
-                collective_id=0, has_side_effects=True, vmem_limit_bytes=32 << 20
+                collective_id=0, has_side_effects=True, vmem_limit_bytes=56 << 20
             ),
         )(q, k, v)
 

time: 65 us -> 70 us (1.077)
  Pallas kernels: 60.7 us -> 67.9 us
  local copies, waits for them, and re-layouts: 4.1 us -> 1.97 us
    pallas_call x1, Pallas kernels: 60.7 us -> 67.9 us  [per_device(): pl.pallas_call(functools.partial(kernel, n_inner, n_outer, heads), out_sh...]
    unnamed x7 -> x1, local copies, waits for them, and re-layouts: 4.1 us -> 1.97 us
where the time goes in v2:
time: 70 us; the launch traced here: 69.8 us
  Pallas kernels  67.9 us (97%)
  local copies, waits for them, and re-layouts  1.97 us (3%)
    pallas_call x1, Pallas kernels, per_device(): pl.pallas_call(functools.partial(kernel, n_inner, n_outer, heads), out_sh...  67.9 us
    unnamed x1, local copies, waits for them, and re-layouts  1.97 us

profile of v2, /device:TPU:1, one launch (start us, length us, event | category | flops | bytes accessed | tf_op | source)
XLA Modules:
  0.0 69.8 jit_solution(15580970979174410927)
XLA Ops:
  0.0 67.9 %shard_map.37 = bf16[128,2560]{1,0:T(8,128)(2,1)} custom-call(bf16[128,2560]{1,0:T(8,128)(2,1)} %q_hbm.1, bf16[128,2560]{1,0:T(8,128)(2,1)} %k_hbm.1, bf16[128,2560]{1,0:T(8,128)(2,1)} %v_hbm.1), custom_call_target="tpu_custom_call" | custom-call | tf_op jit(solution)/shard_map/pallas_call | solution.py:212
  67.9 2.0 %copy.5 = bf16[128,2560]{1,0:T(8,128)(2,1)} copy(bf16[128,2560]{1,0:T(8,128)(2,1)} %shard_map.37) | data formatting | bytes 1310720

commit v3 on v2

--- a/solution.py
+++ b/solution.py
@@ -13,6 +13,16 @@
 LANE = 128
 TAIL = 16
 LAG = 2
+BACK, BACK_WRAP = 8, 6
+ORDER_0 = (1, 0, 3, 2, 8, 9, 5, 4, 6, 7)
+PASSES = (
+    (("first", 8, (0, 1, 2, 3)), ("ring", 0, (0,)), ("first", 9, (0,))),
+    (("first", 9, (1, 2, 3)),),
+    (("first", 6, (2,)), ("second", 8, (0, 1, 3)), ("ring", 2, (0,)), ("second", 9, (0,))),
+    (("first", 7, (2,)), ("second", 9, (1, 3))),
+    (("second", 6, (1,)), ("second", 8, (2,))),
+    (("second", 7, (1,)), ("second", 9, (2,)), ("ring", 4, (0,))),
+)
 
 
 def cols(at, count=1):
@@ -49,7 +59,9 @@
     along = n_outer // 2
     side, y = outer // along, lax.rem(outer, along)
     flipped = (1 - side) * along + y
-    ring_up, ring_down = side * along + lax.rem(y + 1, along), side * along + lax.rem(y + along - 1, along)
+    y_up, y_down = lax.rem(y + 1, along), lax.rem(y + along - 1, along)
+    ring_up, ring_down = side * along + y_up, side * along + y_down
+    cross_up, cross_down = (1 - side) * along + y_up, (1 - side) * along + y_down
     kv_far = kv_in.at[0]
     my_rows = pl.ds(pl.multiple_of(core * rows, rows), rows)
 
@@ -63,7 +75,8 @@
     greeted = [(inner, outer, other)]
     for c in range(2):
         greeted += [(inner_up, outer, c), (inner_down, outer, c), (inner, outer_up, c), (inner, outer_down, c)]
-        greeted += [(inner, ring_up, c), (inner, ring_down, c), (inner, flipped, c)]
+        greeted += [(inner, ring_up, c), (inner, ring_down, c)]
+    greeted += [(inner, at, core) for at in (flipped, cross_up, cross_down)]
     for device in greeted:
         pl.semaphore_signal(barrier, inc=1, device_id=device, device_id_type=MESH)
     pl.semaphore_wait(barrier, len(greeted))
@@ -78,20 +91,25 @@
         copy.start()
         swaps.append(copy)
 
-    def send_head(j, _):
+    def send_head(n, _):
+        late = jnp.where(n == heads - 1, 5, BACK_WRAP + lax.rem(n // 2 + 2, heads - BACK_WRAP))
+        last = y == along - 1
+        j = jnp.where(last, jnp.where(lax.rem(n, 2) == 0, n // 2, late), lax.rem(n + BACK, heads))
         for c in range(2):
             pltpu.make_async_remote_copy(
                 src_ref=q_hbm.at[:, cols(c * heads + j)], dst_ref=q_all.at[1, my_rows, cols(j)],
                 send_sem=q_send, recv_sem=q_recv.at[j],
                 device_id=(inner_down, outer, c), device_id_type=MESH,
             ).start()
-        by_ring = jnp.where((y == along - 1) & (lax.rem(j, 2) == 0), 1, 0)
-        target = jnp.where(by_ring == 1, ring_up, outer_up)
+        back = jnp.where(j >= BACK, 1, jnp.where(last & (j >= BACK_WRAP), 1, 0))
+        by_ring = jnp.where(last & (back == 0) & (lax.rem(j, 2) == 0), 1, 0)
+        target = jnp.where(back == 1, ring_down, jnp.where(by_ring == 1, ring_up, outer_up))
+        place = back + by_ring
         for at, src in enumerate((k_hbm, v_hbm)):
             for c in range(2):
                 pltpu.make_async_remote_copy(
-                    src_ref=src.at[:, cols(c * heads + j)], dst_ref=kv_in.at[by_ring, at, my_rows, cols(j)],
-                    send_sem=kv_send.at[at], recv_sem=kv_recv.at[by_ring, j],
+                    src_ref=src.at[:, cols(c * heads + j)], dst_ref=kv_in.at[place, at, my_rows, cols(j)],
+                    send_sem=kv_send.at[at], recv_sem=kv_recv.at[place, j],
                     device_id=(inner, target, c), device_id_type=MESH,
                 ).start()
         return 0
@@ -145,16 +163,37 @@
             result[:, cols(g)] = mixed.T.astype(jnp.bfloat16)
             pltpu.make_async_copy(result.at[:, cols(g)], o_hbm.at[:, cols(g)], out_sem).start()
 
-    def head_step(j, _):
-        @pl.when((y == 0) & (lax.rem(j, 2) == 0))
-        def _():
-            passing = kv_in.at[1, :, :, cols(j)]
-            pltpu.make_async_copy(passing, passing, kv_recv.at[1, j]).wait()
-            pltpu.make_async_remote_copy(
-                src_ref=passing, dst_ref=kv_far.at[:, :, cols(j)], send_sem=pass_send, recv_sem=kv_recv.at[0, j],
-                device_id=(inner, flipped, core), device_id_type=MESH,
-            ).start()
-
+    def pass_on(kind, j):
+        source, place, target = {
+            "first": (1, 2, ring_down if j % 2 else jnp.where(y == 2, cross_down, ring_down)),
+            "second": (2, 0, jnp.where(y == 1, cross_down, ring_down) if j % 2 else ring_down),
+            "ring": (1, 0, flipped),
+        }[kind]
+        block = kv_in.at[source, :, :, cols(j)]
+        pltpu.make_async_copy(block, block, kv_recv.at[source, j]).wait()
+        pltpu.make_async_remote_copy(
+            src_ref=block, dst_ref=kv_in.at[place, :, :, cols(j)], send_sem=pass_send, recv_sem=kv_recv.at[place, j],
+            device_id=(inner, target, core), device_id_type=MESH,
+        ).start()
+
+    def head_at(n):
+        first = ORDER_0[0]
+        for at, j in enumerate(ORDER_0):
+            first = jnp.where(n == at, j, first)
+        return jnp.where(y == 0, first, n)
+
+    def head_step(n, _):
+        for at, passes in enumerate(PASSES):
+
+            @pl.when(n == at)
+            def _():
+                for kind, which, ys in passes:
+
+                    @pl.when(functools.reduce(jnp.logical_or, [y == own_y for own_y in ys]))
+                    def _():
+                        pass_on(kind, which)
+
+        j = head_at(n)
         pltpu.make_async_copy(q_all.at[1, :, cols(j)], q_all.at[1, :, cols(j)], q_recv.at[j]).wait()
         pltpu.make_async_copy(kv_far.at[:, :, cols(j)], kv_far.at[:, :, cols(j)], kv_recv.at[0, j]).wait()
         g = core * heads + j
@@ -177,15 +216,15 @@
         ).start()
         part_own[g] = o_mine[j, :, halves(core)]
 
-        @pl.when(j >= LAG)
+        @pl.when(n >= LAG)
         def _():
-            merge(j - LAG)
+            merge(head_at(n - LAG))
 
         return 0
 
     lax.fori_loop(0, heads, head_step, 0)
-    for j in range(heads - LAG, heads):
-        merge(j)
+    for n in range(heads - LAG, heads):
+        merge(head_at(n))
 
     pltpu.make_async_copy(result, o_hbm, out_sem).wait()
     pltpu.make_async_copy(q_hbm, q_hbm, q_send).wait()
@@ -193,10 +232,13 @@
     pltpu.make_async_copy(v_hbm, v_hbm, kv_send.at[1]).wait()
     pltpu.make_async_copy(o_out, o_out, far_send).wait()
 
-    @pl.when(y == 0)
-    def _():
-        passed = kv_in.at[1, :, :, cols(0, (heads + 1) // 2)]
-        pltpu.make_async_copy(passed, passed, pass_send).wait()
+    for own_y in range(along):
+        count = sum(own_y in ys for passes in PASSES for _, _, ys in passes)
+
+        @pl.when(y == own_y)
+        def _():
+            passed = kv_in.at[1, :, :, cols(0, count)]
+            pltpu.make_async_copy(passed, passed, pass_send).wait()
 
     pltpu.make_async_copy(o_mine.at[:, :, halves(0)], o_mine.at[:, :, halves(0)], mine_send).wait()
 
@@ -217,14 +259,14 @@
             scratch_shapes=[
                 pltpu.VMEM((2, both, width // 2), jnp.bfloat16),
                 pltpu.VMEM((2, both, width // 2), jnp.bfloat16),
-                pltpu.VMEM((2, 2, both, width // 2), jnp.bfloat16),
+                pltpu.VMEM((3, 2, both, width // 2), jnp.bfloat16),
                 pltpu.VMEM((heads, HD + TAIL, both), jnp.bfloat16),
                 pltpu.VMEM((heads, HD + TAIL, both), jnp.bfloat16),
                 pltpu.VMEM((2 * heads, HD + TAIL, rows), jnp.bfloat16),
                 pltpu.VMEM((2 * heads, HD + TAIL, rows), jnp.bfloat16),
                 pltpu.VMEM((rows, width), jnp.bfloat16),
                 dma((3,)), dma((3,)), dma((3,)),
-                dma, dma((heads,)), dma((2,)), dma((2, heads)), dma,
+                dma, dma((heads,)), dma((2,)), dma((3, heads)), dma,
                 dma, dma((2 * heads,)), dma, dma((heads,)), dma,
             ],
             compiler_params=pltpu.CompilerParams(

time: 70 us -> 59.2 us (0.85)
  Pallas kernels: 67.9 us -> 56.4 us
    pallas_call x1, Pallas kernels: 67.9 us -> 56.4 us  [per_device(): pl.pallas_call(functools.partial(kernel, n_inner, n_outer, heads), out_sh...]
where the time goes in v3:
time: 59.2 us; the launch traced here: 58.4 us
  Pallas kernels  56.4 us (95%)
  local copies, waits for them, and re-layouts  1.97 us (3%)
    pallas_call x1, Pallas kernels, per_device(): pl.pallas_call(functools.partial(kernel, n_inner, n_outer, heads), out_sh...  56.4 us
    unnamed x1, local copies, waits for them, and re-layouts  1.97 us

profile of v3, /device:TPU:1, one launch (start us, length us, event | category | flops | bytes accessed | tf_op | source)
XLA Modules:
  0.0 58.4 jit_solution(11387461218058086825)
XLA Ops:
  0.0 56.4 %shard_map.37 = bf16[128,2560]{1,0:T(8,128)(2,1)} custom-call(bf16[128,2560]{1,0:T(8,128)(2,1)} %q_hbm.1, bf16[128,2560]{1,0:T(8,128)(2,1)} %k_hbm.1, bf16[128,2560]{1,0:T(8,128)(2,1)} %v_hbm.1), custom_call_target="tpu_custom_call" | custom-call | tf_op jit(solution)/shard_map/pallas_call | solution.py:254
  56.4 2.0 %copy.5 = bf16[128,2560]{1,0:T(8,128)(2,1)} copy(bf16[128,2560]{1,0:T(8,128)(2,1)} %shard_map.37) | data formatting | bytes 1310720

commit v4 on v3

--- a/solution.py
+++ b/solution.py
@@ -12,17 +12,22 @@
 MESH = pl.DeviceIdType.MESH
 LANE = 128
 TAIL = 16
-LAG = 2
-BACK, BACK_WRAP = 8, 6
-ORDER_0 = (1, 0, 3, 2, 8, 9, 5, 4, 6, 7)
+BACK, BACK_WRAP = 8, 5
+EVERY = (0, 1, 2, 3)
 PASSES = (
-    (("first", 8, (0, 1, 2, 3)), ("ring", 0, (0,)), ("first", 9, (0,))),
-    (("first", 9, (1, 2, 3)),),
-    (("first", 6, (2,)), ("second", 8, (0, 1, 3)), ("ring", 2, (0,)), ("second", 9, (0,))),
-    (("first", 7, (2,)), ("second", 9, (1, 3))),
-    (("second", 6, (1,)), ("second", 8, (2,))),
-    (("second", 7, (1,)), ("second", 9, (2,)), ("ring", 4, (0,))),
+    (("first", 8, EVERY), ("first", 9, EVERY)), (("second", 8, (0, 2, 3)),), (("second", 9, (0, 2, 3)),), (("second", 9, (1,)),), (), (("second", 8, (1,)),),
 )
+PASSES_WRAP = (
+    (("first", 8, EVERY), ("ring", 0, (0,)), ("first", 9, EVERY), ("ring", 1, (0,))),
+    (("query", 0, EVERY), ("first", 6, (2,)), ("second", 8, (0, 1, 3)), ("ring", 2, (0,))),
+    (("query", 1, EVERY), ("first", 7, (2,)), ("second", 9, (0, 1, 3)), ("ring", 3, (0,))),
+    (("query", 2, EVERY), ("first", 5, (2,)), ("second", 6, (1,)), ("ring", 4, (0,))),
+    (("second", 8, (2,)), ("second", 7, (1,))),
+    (("second", 9, (2,)), ("second", 5, (1,))),
+)
+HOLD = 3
+HANDED = (0, 4, 7, 10)
+ORDER_WRAP = (0, 1, 2, 8, 3, 9, 6, 4, 7, 5)
 
 
 def cols(at, count=1):
@@ -46,10 +51,10 @@
 
 def kernel(
     n_inner, n_outer, heads,
-    q_hbm, k_hbm, v_hbm, o_hbm,
-    q_all, kv_own, kv_in, o_out, o_mine, part_own, part_far, result,
-    own_sem, swap_send, swap_recv, q_send, q_recv, kv_send, kv_recv, pass_send,
-    far_send, far_recv, mine_send, mine_recv, out_sem,
+    q_hbm, k_hbm, v_hbm, result,
+    q_all, kv_own, kv_in, o_out, o_mine, part_own, part_far,
+    entered, own_sem, swap_send, swap_recv, q_send, q_recv, hand_send, kv_send, kv_recv, pass_send,
+    far_send, far_recv, mine_send, mine_recv,
 ):
     inner, outer, core = lax.axis_index("inner"), lax.axis_index("outer"), lax.axis_index("head")
     rows = q_hbm.shape[0]
@@ -59,6 +64,12 @@
     along = n_outer // 2
     side, y = outer // along, lax.rem(outer, along)
     flipped = (1 - side) * along + y
+    z = lax.rem(inner, n_inner // 2)
+    far = n_inner // 2 - 1
+    wrap = z == 0
+    mate = lax.rem(inner + n_inner // 2, n_inner)
+    below, above = lax.rem(inner + far, n_inner), lax.rem(inner + n_inner - far, n_inner)
+    handing, handed = wrap & (y == along - 1), (z == far) & (y == along - 1)
     y_up, y_down = lax.rem(y + 1, along), lax.rem(y + along - 1, along)
     ring_up, ring_down = side * along + y_up, side * along + y_down
     cross_up, cross_down = (1 - side) * along + y_up, (1 - side) * along + y_down
@@ -72,14 +83,23 @@
         own.append(copy)
 
     barrier = pltpu.get_barrier_semaphore()
-    greeted = [(inner, outer, other)]
+    around = [(inner, outer, other)]
     for c in range(2):
-        greeted += [(inner_up, outer, c), (inner_down, outer, c), (inner, outer_up, c), (inner, outer_down, c)]
-        greeted += [(inner, ring_up, c), (inner, ring_down, c)]
-    greeted += [(inner, at, core) for at in (flipped, cross_up, cross_down)]
-    for device in greeted:
+        around += [(inner, at, c) for at in (outer_up, outer_down, ring_up, ring_down)]
+    around += [(inner, at, core) for at in (flipped, cross_up, cross_down)]
+    for device in around + [(inner_down, outer, c) for c in range(2)]:
         pl.semaphore_signal(barrier, inc=1, device_id=device, device_id_type=MESH)
-    pl.semaphore_wait(barrier, len(greeted))
+
+    @pl.when(handing)
+    def _():
+        for at in (mate, below):
+            for c in range(2):
+                pl.semaphore_signal(barrier, inc=1, device_id=(at, outer, c), device_id_type=MESH)
+
+    pl.semaphore_wait(barrier, len(around) + 2 + jnp.where(handing | handed, 2, 0))
+    for c in range(2):
+        device = (jnp.where(handed, above, inner_up), outer, c)
+        pl.semaphore_signal(entered, inc=1, device_id=device, device_id_type=MESH)
 
     swaps = []
     for at, (src, dst) in enumerate(((q_hbm, q_all.at[0]), (k_hbm, kv_own.at[0]), (v_hbm, kv_own.at[1]))):
@@ -92,17 +112,11 @@
         swaps.append(copy)
 
     def send_head(n, _):
-        late = jnp.where(n == heads - 1, 5, BACK_WRAP + lax.rem(n // 2 + 2, heads - BACK_WRAP))
-        last = y == along - 1
+        late = jnp.where(n == heads - 1, BACK_WRAP, BACK_WRAP + 1 + lax.rem(n // 2 + 2, heads - BACK_WRAP - 1))
+        last = (y == along - 1) & wrap
         j = jnp.where(last, jnp.where(lax.rem(n, 2) == 0, n // 2, late), lax.rem(n + BACK, heads))
-        for c in range(2):
-            pltpu.make_async_remote_copy(
-                src_ref=q_hbm.at[:, cols(c * heads + j)], dst_ref=q_all.at[1, my_rows, cols(j)],
-                send_sem=q_send, recv_sem=q_recv.at[j],
-                device_id=(inner_down, outer, c), device_id_type=MESH,
-            ).start()
         back = jnp.where(j >= BACK, 1, jnp.where(last & (j >= BACK_WRAP), 1, 0))
-        by_ring = jnp.where(last & (back == 0) & (lax.rem(j, 2) == 0), 1, 0)
+        by_ring = jnp.where(last & (back == 0), 1, 0)
         target = jnp.where(back == 1, ring_down, jnp.where(by_ring == 1, ring_up, outer_up))
         place = back + by_ring
         for at, src in enumerate((k_hbm, v_hbm)):
@@ -114,7 +128,36 @@
                 ).start()
         return 0
 
+    q_place, q_target = jnp.where(handing, 2, 1), jnp.where(handing, mate, inner_down)
+
+    def send_query(j, _):
+        for c in range(2):
+            pltpu.make_async_remote_copy(
+                src_ref=q_hbm.at[:, cols(c * heads + j)], dst_ref=q_all.at[q_place, my_rows, cols(j)],
+                send_sem=q_send, recv_sem=q_recv.at[q_place, j],
+                device_id=(q_target, outer, c), device_id_type=MESH,
+            ).start()
+        return 0
+
+    def hand_query(j, _):
+        block = q_all.at[2, :, cols(j)]
+        pltpu.make_async_copy(block, block, q_recv.at[2, j]).wait()
+        pltpu.make_async_remote_copy(
+            src_ref=block, dst_ref=q_all.at[1, :, cols(j)], send_sem=hand_send, recv_sem=q_recv.at[1, j],
+            device_id=(below, outer, core), device_id_type=MESH,
+        ).start()
+        return 0
+
+    @pl.when(handing)
+    def _():
+        lax.fori_loop(0, heads, send_query, 0)
+
     lax.fori_loop(0, heads, send_head, 0)
+
+    @pl.when(z > 0)
+    def _():
+        pl.semaphore_wait(entered, 2)
+        lax.fori_loop(0, heads, send_query, 0)
 
     for copy in own:
         copy.wait()
@@ -161,12 +204,11 @@
                 + part_far[g, :HD, :].astype(jnp.float32) * share_far
             )
             result[:, cols(g)] = mixed.T.astype(jnp.bfloat16)
-            pltpu.make_async_copy(result.at[:, cols(g)], o_hbm.at[:, cols(g)], out_sem).start()
 
     def pass_on(kind, j):
         source, place, target = {
-            "first": (1, 2, ring_down if j % 2 else jnp.where(y == 2, cross_down, ring_down)),
-            "second": (2, 0, jnp.where(y == 1, cross_down, ring_down) if j % 2 else ring_down),
+            "first": (1, 2, jnp.where((y == 2) & wrap if j % 2 else y == 2, cross_down, ring_down)),
+            "second": (2, 0, jnp.where((y == 1) & jnp.logical_not(wrap), cross_down, ring_down) if j % 2 else ring_down),
             "ring": (1, 0, flipped),
         }[kind]
         block = kv_in.at[source, :, :, cols(j)]
@@ -177,35 +219,62 @@
         ).start()
 
     def head_at(n):
-        first = ORDER_0[0]
-        for at, j in enumerate(ORDER_0):
-            first = jnp.where(n == at, j, first)
-        return jnp.where(y == 0, first, n)
+        order = ORDER_WRAP[0]
+        for at, j in enumerate(ORDER_WRAP):
+            order = jnp.where(n == at, j, order)
+        return jnp.where((y == 0) & wrap, order, n)
+
+    def run_passes(passes):
+        for kind, which, ys in passes:
+
+            @pl.when(functools.reduce(jnp.logical_or, [y == own_y for own_y in ys]))
+            def _():
+                if kind != "query":
+                    pass_on(kind, which)
+                    return
+
+                if which == 0:
+                    pl.semaphore_wait(entered, 2)
+
+                    @pl.when(jnp.logical_not(handing))
+                    def _():
+                        lax.fori_loop(0, heads, send_query, 0)
+
+                @pl.when(handing)
+                def _():
+                    lax.fori_loop(HANDED[which], HANDED[which + 1], hand_query, 0)
+
+    def send_part(n, _):
+        j = head_at(n)
+        for c in range(2):
+            pltpu.make_async_remote_copy(
+                src_ref=o_out.at[j, :, halves(c)], dst_ref=part_far.at[core * heads + j],
+                send_sem=far_send, recv_sem=far_recv.at[core * heads + j],
+                device_id=(inner_up, outer, c), device_id_type=MESH,
+            ).start()
+        return 0
 
     def head_step(n, _):
-        for at, passes in enumerate(PASSES):
-
-            @pl.when(n == at)
-            def _():
-                for kind, which, ys in passes:
-
-                    @pl.when(functools.reduce(jnp.logical_or, [y == own_y for own_y in ys]))
-                    def _():
-                        pass_on(kind, which)
+        for table, here in ((PASSES, jnp.logical_not(wrap)), (PASSES_WRAP, wrap)):
+            for at, passes in enumerate(table):
+
+                @pl.when((n == at) & here)
+                def _():
+                    run_passes(passes)
 
         j = head_at(n)
-        pltpu.make_async_copy(q_all.at[1, :, cols(j)], q_all.at[1, :, cols(j)], q_recv.at[j]).wait()
+        pltpu.make_async_copy(q_all.at[1, :, cols(j)], q_all.at[1, :, cols(j)], q_recv.at[1, j]).wait()
         pltpu.make_async_copy(kv_far.at[:, :, cols(j)], kv_far.at[:, :, cols(j)], kv_recv.at[0, j]).wait()
         g = core * heads + j
         block, logs = attend(q_all[1, :, cols(j)], j)
         o_out[j, :HD, :] = block
         o_out[j, HD:, :] = logs
-        for c in range(2):
-            pltpu.make_async_remote_copy(
-                src_ref=o_out.at[j, :, halves(c)], dst_ref=part_far.at[g],
-                send_sem=far_send, recv_sem=far_recv.at[g],
-                device_id=(inner_up, outer, c), device_id_type=MESH,
-            ).start()
+        held = jnp.where(z == far, HOLD, 0)
+
+        @pl.when(n >= held)
+        def _():
+            lax.fori_loop(jnp.where(n == held, 0, n), n + 1, send_part, 0)
+
         block, logs = attend(q_all[0, :, cols(j)], j)
         o_mine[j, :HD, :] = block
         o_mine[j, HD:, :] = logs
@@ -216,29 +285,29 @@
         ).start()
         part_own[g] = o_mine[j, :, halves(core)]
 
-        @pl.when(n >= LAG)
-        def _():
-            merge(head_at(n - LAG))
-
         return 0
 
     lax.fori_loop(0, heads, head_step, 0)
-    for n in range(heads - LAG, heads):
-        merge(head_at(n))
-
-    pltpu.make_async_copy(result, o_hbm, out_sem).wait()
+    lax.fori_loop(0, heads, lambda n, _: merge(n) or 0, 0)
+
     pltpu.make_async_copy(q_hbm, q_hbm, q_send).wait()
+
+    @pl.when(handing)
+    def _():
+        pltpu.make_async_copy(q_all.at[2], q_all.at[2], hand_send).wait()
+
     pltpu.make_async_copy(k_hbm, k_hbm, kv_send.at[0]).wait()
     pltpu.make_async_copy(v_hbm, v_hbm, kv_send.at[1]).wait()
     pltpu.make_async_copy(o_out, o_out, far_send).wait()
 
     for own_y in range(along):
-        count = sum(own_y in ys for passes in PASSES for _, _, ys in passes)
-
-        @pl.when(y == own_y)
-        def _():
-            passed = kv_in.at[1, :, :, cols(0, count)]
-            pltpu.make_async_copy(passed, passed, pass_send).wait()
+        for table, here in ((PASSES, jnp.logical_not(wrap)), (PASSES_WRAP, wrap)):
+            count = sum(own_y in ys for passes in table for kind, _, ys in passes if kind != "query")
+
+            @pl.when((y == own_y) & here)
+            def _():
+                passed = kv_in.at[1, :, :, cols(0, count)]
+                pltpu.make_async_copy(passed, passed, pass_send).wait()
 
     pltpu.make_async_copy(o_mine.at[:, :, halves(0)], o_mine.at[:, :, halves(0)], mine_send).wait()
 
@@ -255,22 +324,21 @@
             functools.partial(kernel, n_inner, n_outer, heads),
             out_shape=jax.ShapeDtypeStruct((rows, width), jnp.bfloat16),
             in_specs=[pl.BlockSpec(memory_space=pltpu.HBM)] * 3,
-            out_specs=pl.BlockSpec(memory_space=pl.ANY),
+            out_specs=pl.BlockSpec(memory_space=pltpu.VMEM),
             scratch_shapes=[
-                pltpu.VMEM((2, both, width // 2), jnp.bfloat16),
+                pltpu.VMEM((3, both, width // 2), jnp.bfloat16),
                 pltpu.VMEM((2, both, width // 2), jnp.bfloat16),
                 pltpu.VMEM((3, 2, both, width // 2), jnp.bfloat16),
                 pltpu.VMEM((heads, HD + TAIL, both), jnp.bfloat16),
                 pltpu.VMEM((heads, HD + TAIL, both), jnp.bfloat16),
                 pltpu.VMEM((2 * heads, HD + TAIL, rows), jnp.bfloat16),
                 pltpu.VMEM((2 * heads, HD + TAIL, rows), jnp.bfloat16),
-                pltpu.VMEM((rows, width), jnp.bfloat16),
-                dma((3,)), dma((3,)), dma((3,)),
-                dma, dma((heads,)), dma((2,)), dma((3, heads)), dma,
-                dma, dma((2 * heads,)), dma, dma((heads,)), dma,
+                pltpu.SemaphoreType.REGULAR, dma((3,)), dma((3,)), dma((3,)),
+                dma, dma((3, heads)), dma, dma((2,)), dma((3, heads)), dma,
+                dma, dma((2 * heads,)), dma, dma((heads,)),
             ],
             compiler_params=pltpu.CompilerParams(
-                collective_id=0, has_side_effects=True, vmem_limit_bytes=56 << 20
+                collective_id=0, has_side_effects=True, vmem_limit_bytes=53 << 20
             ),
         )(q, k, v)
 

time: 59.2 us -> 48.8 us (0.82); the launches traced: 58.4 us -> 48.7 us
  Pallas kernels: 56.4 us -> 47.8 us
  local copies, waits for them, and re-layouts: 1.97 us -> 0.84 us
    pallas_call x1, Pallas kernels: 56.4 us -> 47.8 us  [per_device(): pl.pallas_call(functools.partial(kernel, n_inner, n_outer, heads), out_sh...]
    unnamed x1, local copies, waits for them, and re-layouts: 1.97 us -> 0.84 us
where the time goes in v4:
time: 48.8 us; the launch traced here: 48.7 us
  Pallas kernels  47.8 us (98%)
  local copies, waits for them, and re-layouts  0.84 us (2%)
    pallas_call x1, Pallas kernels, per_device(): pl.pallas_call(functools.partial(kernel, n_inner, n_outer, heads), out_sh...  47.8 us

profile of v4, /device:TPU:1, one launch (start us, length us, event | category | flops | bytes accessed | tf_op | source)
XLA Modules:
  0.0 48.7 jit_solution(1239030301147394769)
XLA Ops:
  0.0 47.8 %shard_map.37 = bf16[128,2560]{1,0:T(8,128)(2,1)S(1)} custom-call(bf16[128,2560]{1,0:T(8,128)(2,1)} %q_hbm.1, bf16[128,2560]{1,0:T(8,128)(2,1)} %k_hbm.1, bf16[128,2560]{1,0:T(8,128)(2,1)} %v_hbm.1), custom_call_target="tpu_custom_call" | custom-call | tf_op jit(solution)/shard_map/pallas_call | solution.py:323
  47.9 0.8 %copy.5 = bf16[128,2560]{1,0:T(8,128)(2,1)} copy(bf16[128,2560]{1,0:T(8,128)(2,1)S(1)} %shard_map.37) | data formatting | bytes 1310720

commit v5 on v4

--- a/solution.py
+++ b/solution.py
@@ -11,22 +11,28 @@
 HD = 128
 MESH = pl.DeviceIdType.MESH
 LANE = 128
-TAIL = 16
+STATS = 16
+EARLY = 8
 BACK, BACK_WRAP = 8, 5
 EVERY = (0, 1, 2, 3)
 PASSES = (
-    (("first", 8, EVERY), ("first", 9, EVERY)), (("second", 8, (0, 2, 3)),), (("second", 9, (0, 2, 3)),), (("second", 9, (1,)),), (), (("second", 8, (1,)),),
+    (("first", 8, EVERY),), (("first", 9, EVERY), ("second", 8, EVERY),), (("second", 9, EVERY),),
+)
+PASSES_FAR = (
+    (("first", 8, EVERY), ("first", 9, EVERY), ("second", 8, (1, 2, 3)), ("second", 9, (1, 2, 3))),
+    (("second", 8, (0,)),), (("second", 9, (0,)),),
 )
 PASSES_WRAP = (
-    (("first", 8, EVERY), ("ring", 0, (0,)), ("first", 9, EVERY), ("ring", 1, (0,))),
-    (("query", 0, EVERY), ("first", 6, (2,)), ("second", 8, (0, 1, 3)), ("ring", 2, (0,))),
-    (("query", 1, EVERY), ("first", 7, (2,)), ("second", 9, (0, 1, 3)), ("ring", 3, (0,))),
-    (("query", 2, EVERY), ("first", 5, (2,)), ("second", 6, (1,)), ("ring", 4, (0,))),
+    (("first", 8, EVERY), ("ring", 0, (0,)), ("first", 9, EVERY), ("query", 0, EVERY), ("ring", 1, (0,))),
+    (("query", 1, EVERY), ("first", 6, (2,)), ("second", 8, (0, 1, 3)), ("ring", 2, (0,))),
+    (("query", 2, EVERY), ("first", 7, (2,)), ("second", 9, (0, 1, 3)), ("ring", 3, (0,))),
+    (("first", 5, (2,)), ("second", 6, (1,)), ("ring", 4, (0,))),
     (("second", 8, (2,)), ("second", 7, (1,))),
     (("second", 9, (2,)), ("second", 5, (1,))),
 )
-HOLD = 3
-HANDED = (0, 4, 7, 10)
+HOLD = (0, 0, 1, 0)
+HANDED = (0, 3, 6, 10)
+ORDER = (0, 1, 2, 3, 4, 8, 5, 9, 6, 7)
 ORDER_WRAP = (0, 1, 2, 8, 3, 9, 6, 4, 7, 5)
 
 
@@ -36,25 +42,14 @@
 
 def halves(at):
     return pl.ds(pl.multiple_of(at * LANE, LANE), LANE)
-
-
-def split_sum(x):
-    high = x.astype(jnp.bfloat16)
-    rest = x - high.astype(jnp.float32)
-    mid = rest.astype(jnp.bfloat16)
-    low = (rest - mid.astype(jnp.float32)).astype(jnp.bfloat16)
-    row = lax.broadcasted_iota(jnp.int32, (TAIL, x.shape[1]), 0)
-    wide = [jnp.broadcast_to(part.astype(jnp.float32), (TAIL, x.shape[1])) for part in (high, mid, low)]
-    tile = jnp.where(row == 0, wide[0], jnp.where(row == 1, wide[1], jnp.where(row == 2, wide[2], 0.0)))
-    return tile.astype(jnp.bfloat16)
 
 
 def kernel(
     n_inner, n_outer, heads,
     q_hbm, k_hbm, v_hbm, result,
-    q_all, kv_own, kv_in, o_out, o_mine, part_own, part_far,
+    q_all, kv_own, kv_in, o_out, o_mine, part_own, part_far, sums_out, sums_mine, sums_own, sums_far,
     entered, own_sem, swap_send, swap_recv, q_send, q_recv, hand_send, kv_send, kv_recv, pass_send,
-    far_send, far_recv, mine_send, mine_recv,
+    far_send, far_recv, mine_send, mine_recv, sums_send, sums_recv, table_sem,
 ):
     inner, outer, core = lax.axis_index("inner"), lax.axis_index("outer"), lax.axis_index("head")
     rows = q_hbm.shape[0]
@@ -69,7 +64,8 @@
     wrap = z == 0
     mate = lax.rem(inner + n_inner // 2, n_inner)
     below, above = lax.rem(inner + far, n_inner), lax.rem(inner + n_inner - far, n_inner)
-    handing, handed = wrap & (y == along - 1), (z == far) & (y == along - 1)
+    by_mate = (y == along - 1) | (y == 1)
+    handing, handed = wrap & by_mate, (z == far) & by_mate
     y_up, y_down = lax.rem(y + 1, along), lax.rem(y + along - 1, along)
     ring_up, ring_down = side * along + y_up, side * along + y_down
     cross_up, cross_down = (1 - side) * along + y_up, (1 - side) * along + y_down
@@ -181,9 +177,10 @@
             )
             for v, w in zip(values, weights)
         )
-        return (summed * (1.0 / total)).astype(jnp.bfloat16), split_sum(top * factor + jnp.log2(total))
-
-    def merge(j):
+        return (summed * (1.0 / total)).astype(jnp.bfloat16), top * factor + jnp.log2(total)
+
+    def merge(n):
+        j = sent_at(n)
         for c in range(2):
             g = c * heads + j
             pltpu.make_async_copy(part_far.at[g], part_far.at[g], far_recv.at[g]).wait()
@@ -191,24 +188,19 @@
         pltpu.make_async_copy(
             part_own.at[other * heads + j], part_own.at[other * heads + j], mine_recv.at[j]
         ).wait()
+        table = jnp.where(n < EARLY, 0, 1)
         for c in range(2):
             g = c * heads + j
-            logs = []
-            for part in (part_own, part_far):
-                tile = part[g, HD:, :].astype(jnp.float32)
-                logs.append(tile[0:1] + tile[1:2] + tile[2:3])
-            share_own = 1.0 / (1.0 + jnp.exp2(logs[1] - logs[0]))
-            share_far = 1.0 / (1.0 + jnp.exp2(logs[0] - logs[1]))
-            mixed = (
-                part_own[g, :HD, :].astype(jnp.float32) * share_own
-                + part_far[g, :HD, :].astype(jnp.float32) * share_far
-            )
+            log_own, log_far = sums_own[c, pl.ds(j, 1), :], sums_far[table, c, pl.ds(j, 1), :]
+            share_own = 1.0 / (1.0 + jnp.exp2(log_far - log_own))
+            share_far = 1.0 / (1.0 + jnp.exp2(log_own - log_far))
+            mixed = part_own[g].astype(jnp.float32) * share_own + part_far[g].astype(jnp.float32) * share_far
             result[:, cols(g)] = mixed.T.astype(jnp.bfloat16)
 
     def pass_on(kind, j):
         source, place, target = {
-            "first": (1, 2, jnp.where((y == 2) & wrap if j % 2 else y == 2, cross_down, ring_down)),
-            "second": (2, 0, jnp.where((y == 1) & jnp.logical_not(wrap), cross_down, ring_down) if j % 2 else ring_down),
+            "first": (1, 2, jnp.where((y == 2) & (wrap if j % 2 else z < far), cross_down, ring_down)),
+            "second": (2, 0, jnp.where((y == 1) & (z > 0 if j % 2 else z == far), cross_down, ring_down)),
             "ring": (1, 0, flipped),
         }[kind]
         block = kv_in.at[source, :, :, cols(j)]
@@ -218,11 +210,28 @@
             device_id=(inner, target, core), device_id_type=MESH,
         ).start()
 
+    def listed(order, n):
+        head = order[0]
+        for at, j in enumerate(order):
+            head = jnp.where(n == at, j, head)
+        return head
+
+    def pick(by_y):
+        return listed(by_y, y)
+
     def head_at(n):
-        order = ORDER_WRAP[0]
-        for at, j in enumerate(ORDER_WRAP):
-            order = jnp.where(n == at, j, order)
-        return jnp.where((y == 0) & wrap, order, n)
+        return jnp.where(wrap, jnp.where(y == 0, listed(ORDER_WRAP, n), n), listed(ORDER, n))
+
+    def sent_at(n):
+        return jnp.where(z == 1, jnp.where(y == 0, listed(ORDER_WRAP, n), n), listed(ORDER, n))
+
+    def send_sums(table):
+        for c in range(2):
+            pltpu.make_async_remote_copy(
+                src_ref=sums_out.at[table, :, halves(c)], dst_ref=sums_far.at[table, core],
+                send_sem=sums_send.at[table], recv_sem=sums_recv.at[table, core],
+                device_id=(inner_up, outer, c), device_id_type=MESH,
+            ).start()
 
     def run_passes(passes):
         for kind, which, ys in passes:
@@ -236,9 +245,9 @@
                 if which == 0:
                     pl.semaphore_wait(entered, 2)
 
-                    @pl.when(jnp.logical_not(handing))
-                    def _():
-                        lax.fori_loop(0, heads, send_query, 0)
+                @pl.when(jnp.logical_not(handing))
+                def _():
+                    lax.fori_loop(HANDED[which], HANDED[which + 1], send_query, 0)
 
                 @pl.when(handing)
                 def _():
@@ -255,7 +264,7 @@
         return 0
 
     def head_step(n, _):
-        for table, here in ((PASSES, jnp.logical_not(wrap)), (PASSES_WRAP, wrap)):
+        for table, here in ((PASSES, (z > 0) & (z < far)), (PASSES_FAR, z == far), (PASSES_WRAP, wrap)):
             for at, passes in enumerate(table):
 
                 @pl.when((n == at) & here)
@@ -267,17 +276,31 @@
         pltpu.make_async_copy(kv_far.at[:, :, cols(j)], kv_far.at[:, :, cols(j)], kv_recv.at[0, j]).wait()
         g = core * heads + j
         block, logs = attend(q_all[1, :, cols(j)], j)
-        o_out[j, :HD, :] = block
-        o_out[j, HD:, :] = logs
-        held = jnp.where(z == far, HOLD, 0)
+        o_out[j] = block
+
+        @pl.when(n < EARLY)
+        def _():
+            sums_out[0, pl.ds(j, 1), :] = logs
+
+        sums_out[1, pl.ds(j, 1), :] = logs
+
+        @pl.when(n == EARLY - 1)
+        def _():
+            send_sums(0)
+
+        @pl.when(n == heads - 1)
+        def _():
+            send_sums(1)
+
+        held = jnp.where(z == far, pick(HOLD), 0)
 
         @pl.when(n >= held)
         def _():
             lax.fori_loop(jnp.where(n == held, 0, n), n + 1, send_part, 0)
 
         block, logs = attend(q_all[0, :, cols(j)], j)
-        o_mine[j, :HD, :] = block
-        o_mine[j, HD:, :] = logs
+        o_mine[j] = block
+        sums_mine[pl.ds(j, 1), :] = logs
         pltpu.make_async_remote_copy(
             src_ref=o_mine.at[j, :, halves(other)], dst_ref=part_own.at[g],
             send_sem=mine_send, recv_sem=mine_recv.at[j],
@@ -288,7 +311,23 @@
         return 0
 
     lax.fori_loop(0, heads, head_step, 0)
-    lax.fori_loop(0, heads, lambda n, _: merge(n) or 0, 0)
+    sums_own[core] = sums_mine[:, halves(core)]
+    swap = pltpu.make_async_remote_copy(
+        src_ref=sums_mine.at[:, halves(other)], dst_ref=sums_own.at[core],
+        send_sem=table_sem.at[0], recv_sem=table_sem.at[1],
+        device_id=(inner, outer, other), device_id_type=MESH,
+    )
+    swap.start()
+    swap.wait()
+
+    def wait_sums(table):
+        for c in range(2):
+            pltpu.make_async_copy(sums_far.at[table, c], sums_far.at[table, c], sums_recv.at[table, c]).wait()
+
+    wait_sums(0)
+    lax.fori_loop(0, EARLY, lambda n, _: merge(n) or 0, 0)
+    wait_sums(1)
+    lax.fori_loop(EARLY, heads, lambda n, _: merge(n) or 0, 0)
 
     pltpu.make_async_copy(q_hbm, q_hbm, q_send).wait()
 
@@ -299,9 +338,12 @@
     pltpu.make_async_copy(k_hbm, k_hbm, kv_send.at[0]).wait()
     pltpu.make_async_copy(v_hbm, v_hbm, kv_send.at[1]).wait()
     pltpu.make_async_copy(o_out, o_out, far_send).wait()
+    for table in range(2):
+        pltpu.make_async_copy(sums_out.at[table], sums_out.at[table], sums_send.at[table]).wait()
+
 
     for own_y in range(along):
-        for table, here in ((PASSES, jnp.logical_not(wrap)), (PASSES_WRAP, wrap)):
+        for table, here in ((PASSES, (z > 0) & (z < far)), (PASSES_FAR, z == far), (PASSES_WRAP, wrap)):
             count = sum(own_y in ys for passes in table for kind, _, ys in passes if kind != "query")
 
             @pl.when((y == own_y) & here)
@@ -329,13 +371,17 @@
                 pltpu.VMEM((3, both, width // 2), jnp.bfloat16),
                 pltpu.VMEM((2, both, width // 2), jnp.bfloat16),
                 pltpu.VMEM((3, 2, both, width // 2), jnp.bfloat16),
-                pltpu.VMEM((heads, HD + TAIL, both), jnp.bfloat16),
-                pltpu.VMEM((heads, HD + TAIL, both), jnp.bfloat16),
-                pltpu.VMEM((2 * heads, HD + TAIL, rows), jnp.bfloat16),
-                pltpu.VMEM((2 * heads, HD + TAIL, rows), jnp.bfloat16),
+                pltpu.VMEM((heads, HD, both), jnp.bfloat16),
+                pltpu.VMEM((heads, HD, both), jnp.bfloat16),
+                pltpu.VMEM((2 * heads, HD, rows), jnp.bfloat16),
+                pltpu.VMEM((2 * heads, HD, rows), jnp.bfloat16),
+                pltpu.VMEM((2, STATS, both), jnp.float32),
+                pltpu.VMEM((STATS, both), jnp.float32),
+                pltpu.VMEM((2, STATS, rows), jnp.float32),
+                pltpu.VMEM((2, 2, STATS, rows), jnp.float32),
                 pltpu.SemaphoreType.REGULAR, dma((3,)), dma((3,)), dma((3,)),
                 dma, dma((3, heads)), dma, dma((2,)), dma((3, heads)), dma,
-                dma, dma((2 * heads,)), dma, dma((heads,)),
+                dma, dma((2 * heads,)), dma, dma((heads,)), dma((2,)), dma((2, 2)), dma((2,)),
             ],
             compiler_params=pltpu.CompilerParams(
                 collective_id=0, has_side_effects=True, vmem_limit_bytes=53 << 20

time: 48.8 us -> 46.5 us (0.953)
  Pallas kernels: 47.8 us -> 45.6 us
    pallas_call x1, Pallas kernels: 47.8 us -> 45.6 us  [per_device(): pl.pallas_call(functools.partial(kernel, n_inner, n_outer, heads), out_sh...]
where the time goes in v5:
time: 46.5 us; the launch traced here: 46.4 us
  Pallas kernels  45.6 us (98%)
  local copies, waits for them, and re-layouts  0.84 us (2%)
    pallas_call x1, Pallas kernels, per_device(): pl.pallas_call(functools.partial(kernel, n_inner, n_outer, heads), out_sh...  45.6 us

profile of v5, /device:TPU:1, one launch (start us, length us, event | category | flops | bytes accessed | tf_op | source)
XLA Modules:
  0.0 46.4 jit_solution(14095410596850433520)
XLA Ops:
  0.0 45.6 %shard_map.37 = bf16[128,2560]{1,0:T(8,128)(2,1)S(1)} custom-call(bf16[128,2560]{1,0:T(8,128)(2,1)} %q_hbm.1, bf16[128,2560]{1,0:T(8,128)(2,1)} %k_hbm.1, bf16[128,2560]{1,0:T(8,128)(2,1)} %v_hbm.1), custom_call_target="tpu_custom_call" | custom-call | tf_op jit(solution)/shard_map/pallas_call | solution.py:365
  45.6 0.8 %copy.5 = bf16[128,2560]{1,0:T(8,128)(2,1)} copy(bf16[128,2560]{1,0:T(8,128)(2,1)S(1)} %shard_map.37) | data formatting | bytes 1310720

commit v6 on v5

--- a/solution.py
+++ b/solution.py
@@ -110,7 +110,7 @@
     def send_head(n, _):
         late = jnp.where(n == heads - 1, BACK_WRAP, BACK_WRAP + 1 + lax.rem(n // 2 + 2, heads - BACK_WRAP - 1))
         last = (y == along - 1) & wrap
-        j = jnp.where(last, jnp.where(lax.rem(n, 2) == 0, n // 2, late), lax.rem(n + BACK, heads))
+        j = jnp.where(last, jnp.where(lax.rem(n, 2) == 0, n // 2, late), jnp.where(n == 0, 0, jnp.where(n <= heads - BACK, n + BACK - 1, n + BACK - heads)))
         back = jnp.where(j >= BACK, 1, jnp.where(last & (j >= BACK_WRAP), 1, 0))
         by_ring = jnp.where(last & (back == 0), 1, 0)
         target = jnp.where(back == 1, ring_down, jnp.where(by_ring == 1, ring_up, outer_up))

time: 46.5 us -> 46.5 us (level)
  no operation moved by 1% of the time
where the time goes in v6:
time: 46.5 us; the launch traced here: 46.4 us
  Pallas kernels  45.6 us (98%)
  local copies, waits for them, and re-layouts  0.84 us (2%)
    pallas_call x1, Pallas kernels, per_device(): pl.pallas_call(functools.partial(kernel, n_inner, n_outer, heads), out_sh...  45.6 us

profile of v6, /device:TPU:1, one launch (start us, length us, event | category | flops | bytes accessed | tf_op | source)
XLA Modules:
  0.0 46.4 jit_solution(156443741849288104)
XLA Ops:
  0.0 45.6 %shard_map.37 = bf16[128,2560]{1,0:T(8,128)(2,1)S(1)} custom-call(bf16[128,2560]{1,0:T(8,128)(2,1)} %q_hbm.1, bf16[128,2560]{1,0:T(8,128)(2,1)} %k_hbm.1, bf16[128,2560]{1,0:T(8,128)(2,1)} %v_hbm.1), custom_call_target="tpu_custom_call" | custom-call | tf_op jit(solution)/shard_map/pallas_call | solution.py:365
  45.6 0.8 %copy.5 = bf16[128,2560]{1,0:T(8,128)(2,1)} copy(bf16[128,2560]{1,0:T(8,128)(2,1)S(1)} %shard_map.37) | data formatting | bytes 1310720

commit v7 on v6

--- a/solution.py
+++ b/solution.py
@@ -81,10 +81,18 @@
     barrier = pltpu.get_barrier_semaphore()
     around = [(inner, outer, other)]
     for c in range(2):
-        around += [(inner, at, c) for at in (outer_up, outer_down, ring_up, ring_down)]
+        around += [(inner, at, c) for at in (outer_up, outer_down)]
     around += [(inner, at, core) for at in (flipped, cross_up, cross_down)]
     for device in around + [(inner_down, outer, c) for c in range(2)]:
         pl.semaphore_signal(barrier, inc=1, device_id=device, device_id_type=MESH)
+
+    ends = (y == 0) | (y == along - 1)
+
+    @pl.when(ends)
+    def _():
+        for c in range(2):
+            device = (inner, jnp.where(y == 0, ring_down, ring_up), c)
+            pl.semaphore_signal(barrier, inc=1, device_id=device, device_id_type=MESH)
 
     @pl.when(handing)
     def _():
@@ -92,7 +100,7 @@
             for c in range(2):
                 pl.semaphore_signal(barrier, inc=1, device_id=(at, outer, c), device_id_type=MESH)
 
-    pl.semaphore_wait(barrier, len(around) + 2 + jnp.where(handing | handed, 2, 0))
+    pl.semaphore_wait(barrier, len(around) + 2 + jnp.where(handing | handed, 2, 0) + jnp.where(ends, 2, 0))
     for c in range(2):
         device = (jnp.where(handed, above, inner_up), outer, c)
         pl.semaphore_signal(entered, inc=1, device_id=device, device_id_type=MESH)

time: 46.5 us -> 46.5 us (level)
  no operation moved by 1% of the time
where the time goes in v7:
time: 46.5 us; the launch traced here: 46.4 us
  Pallas kernels  45.5 us (98%)
  local copies, waits for them, and re-layouts  0.84 us (2%)
    pallas_call x1, Pallas kernels, per_device(): pl.pallas_call(functools.partial(kernel, n_inner, n_outer, heads), out_sh...  45.5 us

profile of v7, /device:TPU:1, one launch (start us, length us, event | category | flops | bytes accessed | tf_op | source)
XLA Modules:
  0.0 46.4 jit_solution(575637040660273437)
XLA Ops:
  0.0 45.5 %shard_map.37 = bf16[128,2560]{1,0:T(8,128)(2,1)S(1)} custom-call(bf16[128,2560]{1,0:T(8,128)(2,1)} %q_hbm.1, bf16[128,2560]{1,0:T(8,128)(2,1)} %k_hbm.1, bf16[128,2560]{1,0:T(8,128)(2,1)} %v_hbm.1), custom_call_target="tpu_custom_call" | custom-call | tf_op jit(solution)/shard_map/pallas_call | solution.py:373
  45.6 0.8 %copy.5 = bf16[128,2560]{1,0:T(8,128)(2,1)} copy(bf16[128,2560]{1,0:T(8,128)(2,1)S(1)} %shard_map.37) | data formatting | bytes 1310720

commit v8 on v5

--- a/solution.py
+++ b/solution.py
@@ -12,7 +12,7 @@
 MESH = pl.DeviceIdType.MESH
 LANE = 128
 STATS = 16
-EARLY = 8
+EARLY = 9
 BACK, BACK_WRAP = 8, 5
 EVERY = (0, 1, 2, 3)
 PASSES = (

time: 46.5 us -> 46.5 us (level)
  no operation moved by 1% of the time
where the time goes in v8:
time: 46.5 us; the launch traced here: 46.4 us
  Pallas kernels  45.6 us (98%)
  local copies, waits for them, and re-layouts  0.84 us (2%)
    pallas_call x1, Pallas kernels, per_device(): pl.pallas_call(functools.partial(kernel, n_inner, n_outer, heads), out_sh...  45.6 us

profile of v8, /device:TPU:1, one launch (start us, length us, event | category | flops | bytes accessed | tf_op | source)
XLA Modules:
  0.0 46.4 jit_solution(1059144828756844566)
XLA Ops:
  0.0 45.6 %shard_map.37 = bf16[128,2560]{1,0:T(8,128)(2,1)S(1)} custom-call(bf16[128,2560]{1,0:T(8,128)(2,1)} %q_hbm.1, bf16[128,2560]{1,0:T(8,128)(2,1)} %k_hbm.1, bf16[128,2560]{1,0:T(8,128)(2,1)} %v_hbm.1), custom_call_target="tpu_custom_call" | custom-call | tf_op jit(solution)/shard_map/pallas_call | solution.py:365
  45.6 0.8 %copy.5 = bf16[128,2560]{1,0:T(8,128)(2,1)} copy(bf16[128,2560]{1,0:T(8,128)(2,1)S(1)} %shard_map.37) | data formatting | bytes 1310720
